TPU v7x, 32 devices: a whole 2x2x4 slice. The times are simulated.
32 devices in a mesh: seq: 8 (over z, y), head: 4 (over x, core).
Axes of the slice: x: 2, y: 2, z: 4, core: 2. Of those that a mesh axis runs over, the one named last changes fastest.
Arguments:
- queries: float32 [768, 1024], P('head', 'seq'), may hold values from -6 to 6
- keys: float32 [768, 1024], P('head', 'seq'), may hold values from -6 to 6
- values: float32 [768, 1024], P('head', 'seq'), may hold values from -6 to 6
- counts: int32 [8], P('seq'), may hold values from 32 to 128
- out_weight: float32 [768, 768], P('head'), may hold values from -0.3125 to 0.3125
- cotangent: float32 [768, 1024], P('head', 'seq'), may hold values from -6 to 6
Outputs:
- output: float32 [768, 1024], P('head', 'seq')
- query_grad: float32 [768, 1024], P('head', 'seq')
- key_grad: float32 [768, 1024], P('head', 'seq')
- value_grad: float32 [768, 1024], P('head', 'seq')
- weight_grad: float32 [768, 768], P('head')
All inputs are finite; a program needn't handle non-finite values.
Results may differ from a plain program's by a relative error of at most 0.0014.
Values sent between devices are 32-bit elements; how exact they have to be, the bound alone decides.
A program may use at most 64 MiB of HBM per device.

v0:
```python
import jax
import jax.numpy as jnp
from jax import lax
from jax.sharding import PartitionSpec as P

HEAD = 64
SPACING_LOCAL = 1
SPACING_CENTRAL = 4
SPACING_WIDE = 16
LOG2_LOCAL = 1
LOG2_CENTRAL = 4


PRECISE = lax.Precision.HIGHEST
MASKED_SCORE = -1e30


def from_partner(shard, axis, apart):
    return lax.ppermute(shard, axis, [(i, i ^ 1 << apart) for i in range(lax.axis_size(axis))])


def pick_rows(block, chooser):
    spacing = chooser.shape[1]
    if spacing == 1:
        return block
    shaped = block.reshape(block.shape[:-1] + (block.shape[-1] // spacing, spacing))
    factor = chooser.reshape((chooser.shape[0],) + (1,) * (block.ndim - 1) + (spacing,))
    return jnp.sum(shaped * factor, axis=-1)


def place_rows(piece, chooser, filler):
    spacing = chooser.shape[1]
    if spacing == 1:
        return piece
    chosen = (chooser > 0.5).reshape((chooser.shape[0],) + (1,) * (piece.ndim - 1) + (spacing,))
    spread = jnp.where(chosen, piece[..., None], filler)
    return spread.reshape(piece.shape[:-1] + (piece.shape[-1] * spacing,))


def scores_of(query_rows, key_rows, key_live, score_scale):
    raw = jnp.einsum("heq,hek->hqk", query_rows, key_rows, precision=PRECISE) * score_scale
    return jnp.where(key_live[:, None, :] > 0.5, raw, MASKED_SCORE)


def segment_rows(bundle, extras, levels):
    for bit_index in range(levels):
        other_bundle, other_extras = from_partner((bundle, extras), "seq", bit_index)
        bundle = jnp.concatenate([bundle, other_bundle], axis=3)
        extras = jnp.concatenate([extras, other_extras], axis=3)
    return (bundle, extras)


def return_terms(terms, levels):
    for bit_index in reversed(range(levels)):
        half = terms.shape[3] // 2
        arrived = from_partner(terms[:, :, :, half:], "seq", bit_index)
        terms = terms[:, :, :, :half] + arrived
    return terms


def key_side(key_own, value_own, own_live, far_query, far_grad, far_lse, far_delta, score_scale):
    scores = scores_of(far_query, key_own, own_live, score_scale)
    probabilities = jnp.exp(scores - far_lse[:, :, None])
    value_part = jnp.einsum("hqk,heq->hek", probabilities, far_grad, precision=PRECISE)
    prob_grads = jnp.einsum("heq,hek->hqk", far_grad, value_own, precision=PRECISE)
    score_grads = probabilities * (prob_grads - far_delta[:, :, None])
    key_part = score_scale * jnp.einsum("hqk,heq->hek", score_grads, far_query, precision=PRECISE)
    return (key_part, value_part)


def segment_grads_of(query_rows, grad_rows, probabilities, score_grads, levels, score_scale):
    key_terms = score_scale * jnp.einsum("hqk,heq->hek", score_grads, query_rows, precision=PRECISE)
    value_terms = jnp.einsum("hqk,heq->hek", probabilities, grad_rows, precision=PRECISE)
    owned = return_terms(jnp.stack([key_terms, value_terms]), levels)
    return (owned[0], owned[1])


def on_device(queries, keys, values, counts, out_weight, cotangent):
    columns, row_count = queries.shape
    local_heads = columns // HEAD
    score_scale = HEAD ** (-0.5)
    shard_levels = lax.axis_size("seq").bit_length() - 1
    branches = (
        (SPACING_LOCAL, min(LOG2_LOCAL, shard_levels)),
        (SPACING_CENTRAL, min(LOG2_CENTRAL, shard_levels)),
    )
    global_heads = lax.axis_index("head") * local_heads + jnp.arange(local_heads, dtype=jnp.int32)
    active_rows = (jnp.arange(row_count, dtype=jnp.int32) < counts[0]).astype(jnp.float32)
    live_heads = jnp.broadcast_to(active_rows[None, :], (local_heads, row_count))
    q_all = queries.reshape(local_heads, HEAD, row_count)
    k_all = keys.reshape(local_heads, HEAD, row_count)
    v_all = values.reshape(local_heads, HEAD, row_count)

    def chooser_for(spacing):
        offsets = global_heads % spacing
        return (jnp.arange(spacing, dtype=jnp.int32)[None, :] == offsets[:, None]).astype(
            jnp.float32
        )

    remembered = []
    out_list = []
    lse_list = []
    for spacing_factor, levels in branches:
        chooser = chooser_for(spacing_factor)
        query_rows = pick_rows(q_all, chooser)
        key_own = pick_rows(k_all, chooser)
        value_own = pick_rows(v_all, chooser)
        own_live = pick_rows(live_heads, chooser)
        pairs, extras = segment_rows(
            jnp.stack([key_own, value_own]), own_live[None, :, None, :], levels
        )
        key_rows = pairs[0]
        value_rows = pairs[1]
        key_live = extras[0, :, 0, :]
        scores = scores_of(query_rows, key_rows, key_live, score_scale)
        row_max = jnp.max(scores, axis=-1)
        weights = jnp.exp(scores - row_max[..., None])
        denominator = jnp.sum(weights, axis=-1)
        branch_out = (
            jnp.einsum("hqk,hek->heq", weights, value_rows, precision=PRECISE)
            / denominator[:, None, :]
        )
        log_total = row_max + jnp.log(denominator)
        out_list.append(place_rows(branch_out, chooser, 0.0))
        lse_list.append(place_rows(log_total, chooser, MASKED_SCORE))
        remembered.append(
            (
                chooser,
                levels,
                query_rows,
                key_own,
                value_own,
                own_live,
                key_rows,
                value_rows,
                key_live,
            )
        )
    far_chooser = chooser_for(SPACING_WIDE)
    far_query = pick_rows(q_all, far_chooser)
    far_key = pick_rows(k_all, far_chooser)
    far_value = pick_rows(v_all, far_chooser)
    far_live = pick_rows(live_heads, far_chooser)
    far_pairs = jnp.stack([far_key, far_value])
    far_extras = far_live[None, :, None, :]
    far_rows = far_query.shape[2]
    running_max = jnp.full((local_heads, far_rows), MASKED_SCORE, jnp.float32)
    pairs_piece = lax.all_gather(far_pairs, "seq", axis=3, tiled=True)
    extras_piece = lax.all_gather(far_extras, "seq", axis=3, tiled=True)
    absorb_scores = scores_of(far_query, pairs_piece[0], extras_piece[0, :, 0, :], score_scale)
    newest = jnp.maximum(running_max, jnp.max(absorb_scores, axis=-1))
    weights = jnp.exp(absorb_scores - newest[..., None])
    summed = jnp.sum(weights, axis=-1)
    gathered = jnp.einsum("hqk,hek->heq", weights, pairs_piece[1], precision=PRECISE)
    out_list.append(place_rows(gathered / summed[:, None, :], far_chooser, 0.0))
    lse_list.append(place_rows(newest + jnp.log(summed), far_chooser, MASKED_SCORE))
    stacked = jnp.stack(lse_list)
    row_peak = jnp.max(stacked, axis=0)
    combined_lse = row_peak + jnp.log(jnp.sum(jnp.exp(stacked - row_peak[None]), axis=0))
    combined = jnp.zeros((local_heads, HEAD, row_count), jnp.float32)
    for spread_lse, spread_out in zip(lse_list, out_list):
        combined = combined + jnp.exp(spread_lse - combined_lse)[:, None, :] * spread_out
    attended = (combined * active_rows[None, None, :]).reshape(columns, row_count)
    terms = lax.dot_general(
        out_weight,
        attended,
        (((0,), (0,)), ((), ())),
        precision=PRECISE,
        preferred_element_type=jnp.float32,
    )
    output = lax.psum_scatter(terms, "head", scatter_dimension=0, tiled=True)
    full_grad = lax.all_gather(cotangent, "head", axis=0, tiled=True)
    grad_attended = jnp.dot(
        out_weight, full_grad, precision=PRECISE, preferred_element_type=jnp.float32
    )
    weight_local = lax.dot_general(
        attended,
        full_grad,
        (((1,), (1,)), ((), ())),
        precision=PRECISE,
        preferred_element_type=jnp.float32,
    )
    weight_grad = lax.psum(weight_local, "seq")
    grad_all = grad_attended.reshape(local_heads, HEAD, row_count) * active_rows[None, None, :]
    delta_all = jnp.sum(grad_all * combined, axis=1)
    query_grad = jnp.zeros((local_heads, HEAD, row_count), jnp.float32)
    key_grad = jnp.zeros((local_heads, HEAD, row_count), jnp.float32)
    value_grad = jnp.zeros((local_heads, HEAD, row_count), jnp.float32)
    for (
        chooser,
        levels,
        query_rows,
        key_own,
        value_own,
        own_live,
        key_rows,
        value_rows,
        key_live,
    ) in remembered:
        grad_rows = pick_rows(grad_all, chooser)
        lse_rows = pick_rows(combined_lse, chooser)
        delta_rows = pick_rows(delta_all, chooser)
        scores = scores_of(query_rows, key_rows, key_live, score_scale)
        probabilities = jnp.exp(scores - lse_rows[:, :, None])
        prob_grads = jnp.einsum("heq,hek->hqk", grad_rows, value_rows, precision=PRECISE)
        score_grads = probabilities * (prob_grads - delta_rows[:, :, None])
        query_part = score_scale * jnp.einsum(
            "hqk,hek->heq", score_grads, key_rows, precision=PRECISE
        )
        key_part, value_part = segment_grads_of(
            query_rows, grad_rows, probabilities, score_grads, levels, score_scale
        )
        query_grad = query_grad + place_rows(query_part, chooser, 0.0)
        key_grad = key_grad + place_rows(key_part, chooser, 0.0)
        value_grad = value_grad + place_rows(value_part, chooser, 0.0)
    far_grad = pick_rows(grad_all, far_chooser)
    far_lse = pick_rows(combined_lse, far_chooser)
    far_delta = pick_rows(delta_all, far_chooser)
    pairs_piece = lax.all_gather(far_pairs, "seq", axis=3, tiled=True)
    extras_piece = lax.all_gather(far_extras, "seq", axis=3, tiled=True)
    scores = scores_of(far_query, pairs_piece[0], extras_piece[0, :, 0, :], score_scale)
    probabilities = jnp.exp(scores - far_lse[:, :, None])
    prob_grads = jnp.einsum("heq,hek->hqk", far_grad, pairs_piece[1], precision=PRECISE)
    score_grads = probabilities * (prob_grads - far_delta[:, :, None])
    far_query_part = score_scale * jnp.einsum(
        "hqk,hek->heq", score_grads, pairs_piece[0], precision=PRECISE
    )
    far_bundle = jnp.stack([far_query, far_grad])
    far_stats = jnp.stack([far_lse, far_delta])[:, :, None, :]
    bundle_piece = lax.all_gather(far_bundle, "seq", axis=3, tiled=True)
    stats_piece = lax.all_gather(far_stats, "seq", axis=3, tiled=True)
    key_part, value_part = key_side(
        far_key,
        far_value,
        far_live,
        bundle_piece[0],
        bundle_piece[1],
        stats_piece[0, :, 0, :],
        stats_piece[1, :, 0, :],
        score_scale,
    )
    query_grad = query_grad + place_rows(far_query_part, far_chooser, 0.0)
    key_grad = key_grad + place_rows(key_part, far_chooser, 0.0)
    value_grad = value_grad + place_rows(value_part, far_chooser, 0.0)
    return (
        output,
        query_grad.reshape(columns, row_count),
        key_grad.reshape(columns, row_count),
        value_grad.reshape(columns, row_count),
        weight_grad,
    )


def solution(mesh):
    in_specs = (
        P("head", "seq"),
        P("head", "seq"),
        P("head", "seq"),
        P("seq"),
        P("head", None),
        P("head", "seq"),
    )
    out_specs = (
        P("head", "seq"),
        P("head", "seq"),
        P("head", "seq"),
        P("head", "seq"),
        P("head", None),
    )
    return jax.shard_map(
        on_device, mesh=mesh, in_specs=in_specs, out_specs=out_specs, check_vma=False
    )
```

profile of v0, /device:TPU:0, one launch (start us, length us, event | category | flops | bytes accessed | tf_op | source)
XLA Modules:
  0.0 281.7 jit_solution(18090613571069340358)
XLA Ops:
  9.4 3.0 %collective-permute-start = (f32[1,3,1,128]{3,1,2,0:T(4,128)}, f32[1,3,1,128]{3,1,2,0:T(4,128)}, u32[]{:S(2)}, u32[]{:S(2)}) collective-permute-start(f32[1,3,1,128]{3,1,2,0:T(4,128)} %broadcast_in_dim_broadcast_in_dim.2), channel_id=1, source_target_pairs={{0,4},{4,0},{8,12},{12,8},{16,20},{20,16},{24,28},{28,24},{1,5},{5... | collective-permute-start | bytes 4616 | tf_op jit(solution)/shard_map/ppermute | solution.py:19
  14.2 1.7 pad_maximum_fusion.4
  15.9 2.0 collective-permute-start.1
  20.2 6.4 %all_gather.19 = f32[768,128]{1,0:T(8,128)S(1)} all-gather(f32[192,128]{1,0:T(8,128)S(1)} %copy-done.18), channel_id=1, replica_groups=mesh['seq'=8,'head'=4] {'head'}, dimensions={0}, use_global_device_ids=true | all-gather | bytes 491520 | tf_op jit(solution)/shard_map/all_gather | solution.py:172
  27.5 1.1 multiply_reduce_fusion.1
  33.0 26.3 %all-gather.2 = f32[8,8,3]{1,2,0:T(4,128)S(1)} all-gather(f32[1,8,3]{1,2,0:T(4,128)S(1)} %bitcast.193), channel_id=2, replica_groups=mesh['seq'=8,'head'=4] {'seq'}, dimensions={0}, use_global_device_ids=true | all-gather | bytes 864 | tf_op jit(solution)/shard_map/all_gather | solution.py:149
  60.5 30.7 %all_gather.18 = f32[2,3,64,64]{2,0,1,3:T(2,128)S(1)} all-gather(f32[2,3,64,8]{2,0,1,3:T(2,128)S(1)} %copy.187), channel_id=1, replica_groups=mesh['seq'=8,'head'=4] {'seq'}, dimensions={3}, use_global_device_ids=true | all-gather | bytes 110592 | tf_op jit(solution)/shard_map/all_gather | solution.py:148
  92.4 30.7 %all_gather.20 = f32[2,3,64,64]{2,0,1,3:T(2,128)S(1)} all-gather(f32[2,3,64,8]{2,0,1,3:T(2,128)S(1)} %copy.209), channel_id=1, replica_groups=mesh['seq'=8,'head'=4] {'seq'}, dimensions={3}, use_global_device_ids=true | all-gather | bytes 110592 | tf_op jit(solution)/shard_map/all_gather | solution.py:230
  131.2 1.1 collective-permute-start.4
  134.1 1.6 collective-permute-done.4
  136.4 2.4 collective-permute-done.6
  139.0 1.9 collective-permute-start.7
  142.9 4.9 %collective-permute-done.7 = f32[2,3,64,128]{3,2,1,0:T(8,128)S(1)} collective-permute-done((f32[2,3,64,128]{3,2,1,0:T(8,128)S(1)}, f32[2,3,64,128]{3,2,1,0:T(8,128)S(1)}, u32[]{:S(2)}, u32[]{:S(2)}) %collective-permute-start.7) | collective-permute-done | bytes 196640 | tf_op jit(solution)/shard_map/ppermute | solution.py:19
  154.2 1.1 multiply_reduce_fusion.8
  162.0 30.8 %all-gather.1 = f32[2,3,64]{1,0,2:T(2,128)S(1)} all-gather(f32[2,3,8]{1,0,2:T(2,128)S(1)} %copy.212), channel_id=3, replica_groups=mesh['seq'=8,'head'=4] {'seq'}, dimensions={2}, use_global_device_ids=true | all-gather | bytes 1728 | tf_op jit(solution)/shard_map/all_gather | solution.py:231
  196.9 1.5 fusion.82
  204.1 1.0 fusion.5
  205.1 1.6 collective-permute-done.9
  206.8 1.8 collective-permute-start.10
  209.1 6.5 %collective-permute-done.10 = f32[2,3,64,64]{3,2,1,0:T(8,128)S(1)} collective-permute-done((f32[2,3,64,64]{3,2,1,0:T(8,128)S(1)}, f32[2,3,64,64]{3,2,1,0:T(8,128)S(1)}, u32[]{:S(2)}, u32[]{:S(2)}) %collective-permute-start.10) | collective-permute-done | bytes 98336 | tf_op jit(solution)/shard_map/ppermute | solution.py:19
  215.8 2.3 collective-permute-start.11
  218.3 3.4 %collective-permute-done.11 = f32[2,3,64,32]{3,2,1,0:T(8,128)S(1)} collective-permute-done((f32[2,3,64,32]{3,2,1,0:T(8,128)S(1)}, f32[2,3,64,32]{3,2,1,0:T(8,128)S(1)}, u32[]{:S(2)}, u32[]{:S(2)}) %collective-permute-start.11) | collective-permute-done | bytes 49184 | tf_op jit(solution)/shard_map/ppermute | solution.py:19
  224.6 47.7 %all-reduce.2.cloned.1.call-done = f32[192,768]{1,0:T(8,128)} async-done(((f32[192,768]{1,0:T(8,128)}), f32[192,768]{1,0:T(8,128)}) %all-reduce.2.cloned.1.call-update) | async-done | bytes 589840 | tf_op jit(solution)/shard_map/psum | solution.py:183
  272.3 1.9 copy.261
  (287 shorter events, 51.3 us)
Async XLA Ops:
  8.0 18.7 %copy-start = (f32[192,768]{1,0:T(8,128)S(1)}, f32[192,768]{1,0:T(8,128)}, u32[]{:S(2)}) copy-start(f32[192,768]{1,0:T(8,128)} %param.10) | copy-start | bytes 1769476
  8.0 264.3 %all-reduce.2.cloned.1.call-start = ((), (), s32[]{:S(2)}) async-start(), calls=%async_computation.1 | async-start | bytes 1179648 | tf_op jit(solution)/shard_map/psum | solution.py:183
  9.4 122.9 %collective-permute-start = (f32[1,3,1,128]{3,1,2,0:T(4,128)}, f32[1,3,1,128]{3,1,2,0:T(4,128)}, u32[]{:S(2)}, u32[]{:S(2)}) collective-permute-start(f32[1,3,1,128]{3,1,2,0:T(4,128)} %broadcast_in_dim_broadcast_in_dim.2), channel_id=1, source_target_pairs={{0,4},{4,0},{8,12},{12,8},{16,20},{20,16},{24,28},{28,24},{1,5},{5... | collective-permute-start | bytes 4616 | tf_op jit(solution)/shard_map/ppermute | solution.py:19
  14.2 111.6 %collective-permute-start.2 = (f32[1,3,1,32]{3,1,2,0:T(4,128)}, f32[1,3,1,32]{3,1,2,0:T(4,128)}, u32[]{:S(2)}, u32[]{:S(2)}) collective-permute-start(f32[1,3,1,32]{3,1,2,0:T(4,128)} %bitcast.7), channel_id=1, source_target_pairs={{0,4},{4,0},{8,12},{12,8},{16,20},{20,16},{24,28},{28,24},{1,5},{5... | collective-permute-start | bytes 1160 | tf_op jit(solution)/shard_map/ppermute | solution.py:19
  14.2 3.7 %copy-start.1 = (f32[192,128]{1,0:T(8,128)S(1)}, f32[192,128]{1,0:T(8,128)}, u32[]{:S(2)}) copy-start(f32[192,128]{1,0:T(8,128)} %param.7) | copy-start | bytes 294916
  15.9 2.1 copy-start.2
  15.9 125.0 %collective-permute-start.1 = (f32[2,3,64,128]{3,2,1,0:T(8,128)}, f32[2,3,64,128]{3,2,1,0:T(8,128)}, u32[]{:S(2)}, u32[]{:S(2)}) collective-permute-start(f32[2,3,64,128]{3,2,1,0:T(8,128)} %pad_maximum_fusion.4), channel_id=1, source_target_pairs={{0,4},{4,0},{8,12},{12,8},{16,20},{20,16},{24,28},{28,24},{1,5},{5... | collective-permute-start | bytes 589832 | tf_op jit(solution)/shard_map/ppermute | solution.py:19
  29.5 103.5 %collective-permute-start.5 = (f32[2,3,64,32]{3,2,1,0:T(8,128)}, f32[2,3,64,32]{3,2,1,0:T(8,128)S(1)}, u32[]{:S(2)}, u32[]{:S(2)}) collective-permute-start(f32[2,3,64,32]{3,2,1,0:T(8,128)} %pad_maximum_fusion.5), channel_id=1, source_target_pairs={{0,4},{4,0},{8,12},{12,8},{16,20},{20,16},{24,28},{28,24},{1,5},{5... | collective-permute-start | bytes 147464 | tf_op jit(solution)/shard_map/ppermute | solution.py:19
  30.4 2.0 copy-start.26
  30.4 61.5 %copy-start.51 = (pred[3,16]{1,0:T(4,128)(4,1)}, pred[3,16]{1,0:T(4,128)(4,1)S(1)}, u32[]{:S(2)}) copy-start(pred[3,16]{1,0:T(4,128)(4,1)S(1)} %get-tuple-element.63) | copy-start | bytes 148
  126.6 3.8 %collective-permute-start.3 = (f32[1,3,1,64]{3,1,2,0:T(4,128)S(1)}, f32[1,3,1,64]{3,1,2,0:T(4,128)S(1)}, u32[]{:S(2)}, u32[]{:S(2)}) collective-permute-start(f32[1,3,1,64]{3,1,2,0:T(4,128)S(1)} %pad_maximum_fusion.11), channel_id=1, source_target_pairs={{0,8},{4,12},{8,0},{12,4},{16,24},{20,28},{24,16},{28,20},{1,9},{5... | collective-permute-start | bytes 2312 | tf_op jit(solution)/shard_map/ppermute | solution.py:19
  131.2 4.5 %collective-permute-start.4 = (f32[1,3,1,128]{3,1,2,0:T(4,128)S(1)}, f32[1,3,1,128]{3,1,2,0:T(4,128)S(1)}, u32[]{:S(2)}, u32[]{:S(2)}) collective-permute-start(f32[1,3,1,128]{3,1,2,0:T(4,128)S(1)} %pad_maximum_fusion.12), channel_id=1, source_target_pairs={{0,16},{4,20},{8,24},{12,28},{16,0},{20,4},{24,8},{28,12},{1,17},{... | collective-permute-start | bytes 4616 | tf_op jit(solution)/shard_map/ppermute | solution.py:19
  133.0 9.7 %copy-start.28 = (pred[3,256]{1,0:T(4,128)(4,1)}, pred[3,256]{1,0:T(4,128)(4,1)S(1)}, u32[]{:S(2)}) copy-start(pred[3,256]{1,0:T(4,128)(4,1)S(1)} %fusion.68) | copy-start | bytes 2308
  133.1 5.7 %collective-permute-start.6 = (f32[2,3,64,64]{3,2,1,0:T(8,128)S(1)}, f32[2,3,64,64]{3,2,1,0:T(8,128)S(1)}, u32[]{:S(2)}, u32[]{:S(2)}) collective-permute-start(f32[2,3,64,64]{3,2,1,0:T(8,128)S(1)} %pad_maximum_fusion.6), channel_id=1, source_target_pairs={{0,8},{4,12},{8,0},{12,4},{16,24},{20,28},{24,16},{28,20},{1,9},{5... | collective-permute-start | bytes 294920 | tf_op jit(solution)/shard_map/ppermute | solution.py:19
  136.4 12.2 %copy-start.32 = (pred[3,256]{1,0:T(4,128)(4,1)}, pred[3,256]{1,0:T(4,128)(4,1)S(1)}, u32[]{:S(2)}) copy-start(pred[3,256]{1,0:T(4,128)(4,1)S(1)} %fusion.69) | copy-start | bytes 2308
  139.0 8.8 %collective-permute-start.7 = (f32[2,3,64,128]{3,2,1,0:T(8,128)S(1)}, f32[2,3,64,128]{3,2,1,0:T(8,128)S(1)}, u32[]{:S(2)}, u32[]{:S(2)}) collective-permute-start(f32[2,3,64,128]{3,2,1,0:T(8,128)S(1)} %pad_maximum_fusion.7), channel_id=1, source_target_pairs={{0,16},{4,20},{8,24},{12,28},{16,0},{20,4},{24,8},{28,12},{1,17},{... | collective-permute-start | bytes 589832 | tf_op jit(solution)/shard_map/ppermute | solution.py:19
  142.7 7.7 %copy-start.34 = (f32[3,128]{1,0:T(4,128)}, f32[3,128]{1,0:T(4,128)S(1)}, u32[]{:S(2)}) copy-start(f32[3,128]{1,0:T(4,128)S(1)} %get-tuple-element.71) | copy-start | bytes 4612
  142.9 7.5 %copy-start.48 = (f32[3,128]{1,0:T(4,128)}, f32[3,128]{1,0:T(4,128)S(1)}, u32[]{:S(2)}) copy-start(f32[3,128]{1,0:T(4,128)S(1)} %fusion.19) | copy-start | bytes 4612
  142.9 5.2 %copy-start.5 = (f32[3,64,32]{1,0,2:T(4,128)S(1)}, f32[3,64,32]{1,0,2:T(4,128)}, u32[]{:S(2)}) copy-start(f32[3,64,32]{1,0,2:T(4,128)} %get-tuple-element.36) | copy-start | bytes 73732
  198.4 73.9 %reduce-scatter.4.cloned.1.call-start = ((), (), s32[]{:S(2)}) async-start(), calls=%async_computation.2 | async-start | bytes 491520
  199.1 7.6 %collective-permute-start.9 = (f32[2,3,64,128]{3,2,1,0:T(8,128)}, f32[2,3,64,128]{3,2,1,0:T(8,128)S(1)}, u32[]{:S(2)}, u32[]{:S(2)}) collective-permute-start(f32[2,3,64,128]{3,2,1,0:T(8,128)} %pad_maximum_fusion.2), channel_id=1, source_target_pairs={{0,16},{4,20},{8,24},{12,28},{16,0},{20,4},{24,8},{28,12},{1,17},{... | collective-permute-start | bytes 589832 | tf_op jit(solution)/shard_map/ppermute | solution.py:19
  201.1 8.0 %collective-permute-start.8 = (f32[2,3,64,128]{3,2,1,0:T(8,128)}, f32[2,3,64,128]{3,2,1,0:T(8,128)S(1)}, u32[]{:S(2)}, u32[]{:S(2)}) collective-permute-start(f32[2,3,64,128]{3,2,1,0:T(8,128)} %pad_maximum_fusion.3), channel_id=1, source_target_pairs={{0,4},{4,0},{8,12},{12,8},{16,20},{20,16},{24,28},{28,24},{1,5},{5... | collective-permute-start | bytes 589832 | tf_op jit(solution)/shard_map/ppermute | solution.py:19
  206.8 8.8 %collective-permute-start.10 = (f32[2,3,64,64]{3,2,1,0:T(8,128)S(1)}, f32[2,3,64,64]{3,2,1,0:T(8,128)S(1)}, u32[]{:S(2)}, u32[]{:S(2)}) collective-permute-start(f32[2,3,64,64]{3,2,1,0:T(8,128)S(1)} %slice.105), channel_id=1, source_target_pairs={{0,8},{4,12},{8,0},{12,4},{16,24},{20,28},{24,16},{28,20},{1,9},{5... | collective-permute-start | bytes 294920 | tf_op jit(solution)/shard_map/ppermute | solution.py:19
  215.8 5.9 %collective-permute-start.11 = (f32[2,3,64,32]{3,2,1,0:T(8,128)S(1)}, f32[2,3,64,32]{3,2,1,0:T(8,128)S(1)}, u32[]{:S(2)}, u32[]{:S(2)}) collective-permute-start(f32[2,3,64,32]{3,2,1,0:T(8,128)S(1)} %slice.107), channel_id=1, source_target_pairs={{0,4},{4,0},{8,12},{12,8},{16,20},{20,16},{24,28},{28,24},{1,5},{5... | collective-permute-start | bytes 147464 | tf_op jit(solution)/shard_map/ppermute | solution.py:19
  (51 other events, 37.4 us)
Sparse Core Ops, SparseCore 0:
  198.5 73.7 all-reduce.1
Sparse Core Ops, SparseCore 1:
  203.6 20.9 reduce-scatter.3
where the time goes:
time: 283 us; the launch traced here: 282 us
  blocking collectives  125 us (44%)
  waiting for transfers between devices  68.7 us (24%)
  local copies, waits for them, and re-layouts  31.8 us (11%)
  between operations  17.2 us (6%)
  starting transfers between devices  14.3 us (5%)
  other arithmetic  12.9 us (5%)
  matrix products  12 us (4%)
    psum x1, waiting for transfers between devices, on_device(): weight_grad = lax.psum(weight_local, 'seq')  47.7 us
    all_gather x1, blocking collectives, on_device(): stats_piece = lax.all_gather(far_stats, 'seq', axis=3, tiled=True)  30.8 us
    all_gather x1, blocking collectives, on_device(): pairs_piece = lax.all_gather(far_pairs, 'seq', axis=3, tiled=True)  30.7 us
    all_gather x1, blocking collectives, on_device(): bundle_piece = lax.all_gather(far_bundle, 'seq', axis=3, tiled=True)  30.7 us
    all_gather x1, blocking collectives, on_device(): extras_piece = lax.all_gather(far_extras, 'seq', axis=3, tiled=True)  26.3 us
    ppermute x12, waiting for transfers between devices, from_partner(): lax.ppermute(shard, axis, [(i, i ^ 1 << apart) for i in range(lax.axis_si...  20.9 us
    unnamed x133, local copies, waits for them, and re-layouts  18.3 us
    ppermute x12, starting transfers between devices, from_partner(): lax.ppermute(shard, axis, [(i, i ^ 1 << apart) for i in range(lax.axis_si...  14.3 us
  transfers between devices with their start and end apart: 14, of which 8 were waited for; matrix products, arithmetic and copies ran while one was open for 10% of the time, Pallas kernels for 0%

commit v1 on v0

--- a/solution.py
+++ b/solution.py
@@ -1,6 +1,10 @@
+import functools
+
 import jax
 import jax.numpy as jnp
 from jax import lax
+from jax.experimental import pallas as pl
+from jax.experimental.pallas import tpu as pltpu
 from jax.sharding import PartitionSpec as P
 
 HEAD = 64
@@ -251,7 +255,439 @@
     )
 
 
+MESH = pl.DeviceIdType.MESH
+NN = ((1,), (0,))
+TN = ((0,), (0,))
+NT = ((1,), (1,))
+
+
+def product(a, b, dims):
+    def once(x, y):
+        return lax.dot_general(
+            x, y, (dims, ((), ())), preferred_element_type=jnp.float32
+        )
+
+    a_top, b_top = a.astype(jnp.bfloat16), b.astype(jnp.bfloat16)
+    a_rest = (a - a_top.astype(jnp.float32)).astype(jnp.bfloat16)
+    b_rest = (b - b_top.astype(jnp.float32)).astype(jnp.bfloat16)
+    return once(a_top, b_top) + (once(a_top, b_rest) + once(a_rest, b_top))
+
+
+def fused_kernel(
+    n_seq, n_head,
+    q_hbm, k_hbm, v_hbm, count_ref, w_hbm, cot_hbm,
+    out_ref, dq_ref, dk_ref, dv_ref, dw_ref,
+    q_ref, k_ref, v_ref, w_ref, cot_ref, load_sem, counted, send_ct, recv_ct, send_y, recv_y, w_half,
+    cot_full, near, grads, kvm, qdm, stats, attended, terms, terms_in, local_w, w_in,
+    send_cot, recv_cot, send_near, recv_near, send_kv, recv_kv, send_qd, recv_qd,
+    send_st, recv_st, send_w, recv_w, send_g, recv_g, send_o, recv_o,
+):
+    columns, rows = q_ref.shape
+    heads = columns // HEAD
+    picked = rows // SPACING_CENTRAL
+    n_far = n_seq // 2
+    loads = [
+        pltpu.make_async_copy(src, dst, load_sem.at[i])
+        for i, (src, dst) in enumerate(
+            ((k_hbm, k_ref), (v_hbm, v_ref), (cot_hbm, cot_ref), (q_hbm, q_ref), (w_hbm, w_ref))
+        )
+    ]
+    for load in loads:
+        load.start()
+    scale = HEAD ** (-0.5)
+    me = lax.axis_index("seq")
+    mine = lax.axis_index("head")
+    side, height = me % 2, me // 2
+    partner = me + 1 - 2 * side
+
+    def at(start, size):
+        return pl.ds(pl.multiple_of(start * size, size), size)
+
+    barrier = pltpu.get_barrier_semaphore()
+    for k in range(1, n_seq):
+        pl.semaphore_signal(
+            barrier, inc=1, device_id={"seq": lax.rem(me + k, n_seq)}, device_id_type=MESH
+        )
+    for k in range(1, n_head):
+        pl.semaphore_signal(
+            barrier, inc=1, device_id={"head": lax.rem(mine + k, n_head)}, device_id_type=MESH
+        )
+    offsets = []
+    for h in range(heads):
+        g = mine * heads + h
+        offsets.append((g % SPACING_CENTRAL, g % SPACING_WIDE))
+    pick_row = lax.broadcasted_iota(jnp.int32, (picked, rows), 0)
+    pick_col = lax.broadcasted_iota(jnp.int32, (picked, rows), 1)
+    chooser = [
+        jnp.where(pick_col == SPACING_CENTRAL * pick_row + o, 1.0, 0.0) for o, _ in offsets
+    ]
+    count = jnp.full((picked, rows), count_ref[0], jnp.int32).astype(jnp.float32)
+    lane = lax.broadcasted_iota(jnp.int32, (1, rows), 1)
+    sub = lax.broadcasted_iota(jnp.int32, (rows, 1), 0).astype(jnp.float32)
+    live_row = jnp.where(lane.astype(jnp.float32) < count[0:1, :], 1.0, 0.0)
+    live_col = sub < count[0:1, 0:1]
+
+    def hs(h):
+        return slice(h * HEAD, (h + 1) * HEAD)
+
+    loads[0].wait()
+    loads[1].wait()
+    for h in range(heads):
+        both = jnp.concatenate([k_ref[hs(h), :], v_ref[hs(h), :]], axis=0)
+        kvm[h, at(me, picked), :] = product(chooser[h], both, NT)
+    counted[0, at(me, 8), :] = count[0:8, :]
+    loads[2].wait()
+    loads[3].wait()
+    loads[4].wait()
+    pl.semaphore_wait(barrier, n_seq + n_head - 2)
+
+    def over_seq(k, src, dst, send, recv):
+        return pltpu.make_async_remote_copy(
+            src_ref=src, dst_ref=dst, send_sem=send.at[k], recv_sem=recv.at[k],
+            device_id={"seq": lax.rem(me + k, n_seq)}, device_id_type=MESH,
+        )
+
+    def over_head(k, src, dst, send, recv):
+        return pltpu.make_async_remote_copy(
+            src_ref=src, dst_ref=dst, send_sem=send.at[k], recv_sem=recv.at[k],
+            device_id={"head": lax.rem(mine + k, n_head)}, device_id_type=MESH,
+        )
+
+    def to_partner(k, src):
+        return pltpu.make_async_remote_copy(
+            src_ref=src, dst_ref=near.at[k], send_sem=send_near.at[k],
+            recv_sem=recv_near.at[k], device_id={"seq": partner}, device_id_type=MESH,
+        )
+
+    def source(k):
+        return lax.rem(me + n_seq - k, n_seq)
+
+    def spread(buffer, send, recv, size):
+        out = []
+        for k in range(1, n_seq):
+            block = buffer.at[:, at(me, size), :]
+            copy = over_seq(k, block, block, send, recv)
+            copy.start()
+            out.append(copy)
+        return out
+
+    def gathered(buffer, send, recv, size):
+        for k in range(1, n_seq):
+            block = buffer.at[:, at(source(k), size), :]
+            over_seq(k, block, block, send, recv).wait_recv()
+
+    def level(k):
+        return 2 * lax.rem(height + k, n_far) + side
+
+    def level_from(k):
+        return 2 * lax.rem(height + n_far - k, n_far) + side
+
+    def across(k, block, send, recv):
+        return pltpu.make_async_remote_copy(
+            src_ref=block, dst_ref=block, send_sem=send.at[k], recv_sem=recv.at[k],
+            device_id={"seq": level(k)}, device_id_type=MESH,
+        )
+
+    def beside(k, src, dst, send, recv):
+        return pltpu.make_async_remote_copy(
+            src_ref=src, dst_ref=dst, send_sem=send.at[n_far + k], recv_sem=recv.at[n_far + k],
+            device_id={"seq": partner}, device_id_type=MESH,
+        )
+
+    def piece(buffer, owner):
+        return buffer.at[:, at(owner, picked), :]
+
+    def begin(buffer, send, recv):
+        own = piece(buffer, me)
+        out = [across(k, own, send, recv) for k in range(1, n_far)]
+        out.append(beside(0, own, own, send, recv))
+        for copy in out:
+            copy.start()
+        return out
+
+    def forward(buffer, send, recv):
+        out = []
+        for k in range(1, n_far):
+            block = piece(buffer, level_from(k))
+            across(k, block, send, recv).wait_recv()
+            copy = beside(k, block, block, send, recv)
+            copy.start()
+            out.append(copy)
+        return out
+
+    def finish(buffer, send, recv):
+        for k in range(n_far):
+            owner = level_from(k) + 1 - 2 * side
+            block = piece(buffer, owner)
+            beside(k, block, block, send, recv).wait_recv()
+
+    sent = []
+    for k in range(1, n_head):
+        copy = over_head(k, cot_ref, cot_full.at[at(mine, columns), :], send_cot, recv_cot)
+        copy.start()
+        sent.append(copy)
+    sent += begin(kvm, send_kv, recv_kv)
+    sent += spread(counted, send_ct, recv_ct, 8)
+    near_copies = [to_partner(0, k_ref), to_partner(1, v_ref), to_partner(2, q_ref)]
+    near_copies[0].start()
+    near_copies[1].start()
+    cot_full[at(mine, columns), :] = cot_ref[...]
+    for k in range(1, n_head):
+        origin = lax.rem(mine + n_head - k, n_head)
+        over_head(
+            k, cot_ref, cot_full.at[at(origin, columns), :], send_cot, recv_cot
+        ).wait_recv()
+    sent += forward(kvm, send_kv, recv_kv)
+    full = cot_full[...]
+    grads[...] = product(w_ref[...], full, NN) * live_row
+    for h in range(heads):
+        both = jnp.concatenate([q_ref[hs(h), :], grads[hs(h), :]], axis=0)
+        qdm[h, at(me, picked), :] = product(chooser[h], both, NT)
+    sent += begin(qdm, send_qd, recv_qd)
+    near_copies[2].start()
+    near_grads = to_partner(3, grads)
+    near_grads.start()
+
+    finish(kvm, send_kv, recv_kv)
+    gathered(counted, send_ct, recv_ct, 8)
+    near_copies[0].wait_recv()
+    near_copies[1].wait_recv()
+    total = n_seq * picked
+    slot = lax.broadcasted_iota(jnp.int32, (total, 1), 0) % picked
+    counts_mid = jnp.concatenate(
+        [jnp.broadcast_to(counted[0, 8 * i:8 * i + 1, 0:1], (picked, 1)) for i in range(n_seq)],
+        axis=0,
+    )
+    partner_count = counted[0, at(partner, 8), :][0:1, 0:1]
+    live_near = sub < partner_count
+
+    kept = []
+    stat_rows = []
+    delta_rows = []
+    for h in range(heads):
+        o, far = offsets[h]
+        place = SPACING_CENTRAL * slot + o
+        far_slot = jnp.where(place % SPACING_WIDE == far, 1.0, 0.0)
+        live_mid = jnp.where(place.astype(jnp.float32) < counts_mid, 1.0, 0.0)
+        in_mid = jnp.where(lane % SPACING_CENTRAL == o, 1.0, 0.0)
+        in_far = jnp.where(lane % SPACING_WIDE == far, 1.0, 0.0)
+        times = live_mid * (in_mid + far_slot * in_far)
+        q = q_ref[hs(h), :]
+        d = grads[hs(h), :]
+        km = kvm[h, :, 0:HEAD]
+        vm = kvm[h, :, HEAD:2 * HEAD]
+        k0, v0 = k_ref[hs(h), :], v_ref[hs(h), :]
+        k1, v1 = near[0, hs(h), :], near[1, hs(h), :]
+        sm = jnp.where(times > 0.5, product(km, q, NN) * scale, MASKED_SCORE)
+        s0 = jnp.where(live_col, product(k0, q, TN) * scale, MASKED_SCORE)
+        s1 = jnp.where(live_near, product(k1, q, TN) * scale, MASKED_SCORE)
+        peak = jnp.maximum(
+            jnp.max(sm, axis=0, keepdims=True),
+            jnp.maximum(
+                jnp.max(s0, axis=0, keepdims=True), jnp.max(s1, axis=0, keepdims=True)
+            ),
+        )
+        wm = times * jnp.exp(sm - peak)
+        w0 = jnp.exp(s0 - peak)
+        w1 = jnp.exp(s1 - peak)
+        bottom = (
+            jnp.sum(wm, axis=0, keepdims=True)
+            + jnp.sum(w0, axis=0, keepdims=True)
+            + jnp.sum(w1, axis=0, keepdims=True)
+        )
+        inverse = 1.0 / bottom
+        pm, p0, p1 = wm * inverse, w0 * inverse, w1 * inverse
+        result = product(vm, pm, TN) + product(v0, p0, NN) + product(v1, p1, NN)
+        lse = peak + jnp.log(bottom)
+        delta = jnp.sum(d * result, axis=0, keepdims=True)
+        attended[hs(h), :] = result * live_row
+        stat_rows.append(lse)
+        delta_rows.append(delta)
+        kept.append((km, vm, pm, p0, p1, delta, far_slot, in_mid, in_far))
+        if h == 0:
+            sent += forward(qdm, send_qd, recv_qd)
+    stat_slot = lax.broadcasted_iota(jnp.int32, (8, rows), 0)
+    dense = jnp.zeros((8, rows), jnp.float32)
+    for i, row in enumerate(stat_rows + delta_rows):
+        dense = jnp.where(stat_slot == i, row, dense)
+    stats[0, at(me, 8), :] = dense
+    chunk = columns // n_seq
+    local_w[...] = product(attended[...], full, NT)
+    other = 1 - side
+
+    def slab(part, k):
+        return at(part * n_far + lax.rem(height + k, n_far), chunk)
+
+    order = list(range(1, n_far)) + [0]
+    for k in order:
+        copy = beside(k, local_w.at[slab(other, k), :], w_half.at[k], send_y, recv_y)
+        copy.start()
+        sent.append(copy)
+    sent += spread(stats, send_st, recv_st, 8)
+    terms[...] = product(w_ref[...], attended[...], TN)
+    for k in range(1, n_head):
+        copy = over_head(
+            k, terms.at[at(lax.rem(mine + k, n_head), columns), :], terms_in.at[k],
+            send_o, recv_o,
+        )
+        copy.start()
+        sent.append(copy)
+
+    for k in order:
+        beside(k, local_w.at[slab(side, k), :], w_half.at[k], send_y, recv_y).wait_recv()
+        w_half[k] = w_half[k] + local_w[slab(side, k), :]
+        if k > 0:
+            copy = pltpu.make_async_remote_copy(
+                src_ref=w_half.at[k], dst_ref=w_in.at[k], send_sem=send_w.at[k],
+                recv_sem=recv_w.at[k], device_id={"seq": level(k)}, device_id_type=MESH,
+            )
+            copy.start()
+            sent.append(copy)
+
+    near_copies[2].wait_recv()
+    for h in range(heads):
+        km, vm, pm, p0, p1, delta, far_slot, in_mid, in_far = kept[h]
+        d = grads[hs(h), :]
+        q = q_ref[hs(h), :]
+        k0, v0 = k_ref[hs(h), :], v_ref[hs(h), :]
+        k1, v1 = near[0, hs(h), :], near[1, hs(h), :]
+        gm = pm * (product(vm, d, NN) - delta)
+        g0 = p0 * (product(v0, d, TN) - delta)
+        g1 = p1 * (product(v1, d, TN) - delta)
+        dq_ref[hs(h), :] = scale * (
+            product(km, gm, TN) + product(k0, g0, NN) + product(k1, g1, NN)
+        )
+        dk_ref[hs(h), :] = product(q, g0, NT)
+        dv_ref[hs(h), :] = product(d, p0, NT)
+
+    summed = w_half[0]
+    for k in range(1, n_far):
+        pltpu.make_async_remote_copy(
+            src_ref=w_half.at[k], dst_ref=w_in.at[k], send_sem=send_w.at[k],
+            recv_sem=recv_w.at[k], device_id={"seq": level(k)}, device_id_type=MESH,
+        ).wait_recv()
+        summed = summed + w_in[k]
+    dw_ref[slab(side, 0), :] = summed
+    own_slab = dw_ref.at[slab(side, 0), :]
+    starts = [across(k, own_slab, send_g, recv_g) for k in range(1, n_far)]
+    starts.append(beside(0, own_slab, own_slab, send_g, recv_g))
+    for copy in starts:
+        copy.start()
+    sent += starts
+
+    finish(qdm, send_qd, recv_qd)
+    gathered(stats, send_st, recv_st, 8)
+    near_grads.wait_recv()
+    def relay():
+        for k in range(1, n_far):
+            block = dw_ref.at[slab(side, n_far - k), :]
+            across(k, block, send_g, recv_g).wait_recv()
+            copy = beside(k, block, block, send_g, recv_g)
+            copy.start()
+            sent.append(copy)
+
+    if heads < 2:
+        relay()
+    theirs = stats[0, at(partner, 8), :]
+    for h in range(heads):
+        _, _, _, _, _, _, far_slot, in_mid, in_far = kept[h]
+        k0, v0 = k_ref[hs(h), :], v_ref[hs(h), :]
+        q1, d1 = near[2, hs(h), :], near[3, hs(h), :]
+        lse1 = theirs[h:h + 1, :]
+        delta1 = theirs[heads + h:heads + h + 1, :]
+        sx = jnp.where(live_col, product(k0, q1, TN) * scale, MASKED_SCORE)
+        px = jnp.exp(sx - lse1)
+        gx = px * (product(v0, d1, TN) - delta1)
+        qm = qdm[h, :, 0:HEAD]
+        dm = qdm[h, :, HEAD:2 * HEAD]
+        times = live_row * (in_mid + far_slot * in_far)
+        sy = jnp.where(times > 0.5, product(qm, k0, NN) * scale, MASKED_SCORE)
+        lse_col, delta_col = [
+            jnp.concatenate(
+                [
+                    jnp.sum(chooser[h] * stats[0, 8 * i + j:8 * i + j + 1, :], axis=1, keepdims=True)
+                    for i in range(n_seq)
+                ],
+                axis=0,
+            )
+            for j in (h, heads + h)
+        ]
+        py = times * jnp.exp(sy - lse_col)
+        gy = py * (product(dm, v0, NN) - delta_col)
+        dk_ref[hs(h), :] = scale * (
+            dk_ref[hs(h), :] + product(q1, gx, NT) + product(qm, gy, TN)
+        )
+        dv_ref[hs(h), :] = dv_ref[hs(h), :] + product(d1, px, NT) + product(dm, py, TN)
+        if h == heads - 2:
+            relay()
+
+    output = terms[at(mine, columns), :]
+    for k in range(1, n_head):
+        over_head(
+            k, terms.at[at(mine, columns), :], terms_in.at[k], send_o, recv_o
+        ).wait_recv()
+    for k in range(1, n_head):
+        output = output + terms_in[k]
+    out_ref[...] = output
+    for k in range(n_far):
+        block = dw_ref.at[slab(other, n_far - k), :]
+        beside(k, block, block, send_g, recv_g).wait_recv()
+    for copy in near_copies + [near_grads] + sent:
+        copy.wait_send()
+
+
+def fused(n_seq, n_head, queries, keys, values, counts, out_weight, cotangent):
+    columns, rows = queries.shape
+    wide = out_weight.shape[1]
+    heads = columns // HEAD
+    picked = rows // SPACING_CENTRAL
+    chunk = columns // n_seq
+    block = jax.ShapeDtypeStruct((columns, rows), jnp.float32)
+    vmem = pl.BlockSpec(memory_space=pltpu.VMEM)
+    hbm = pl.BlockSpec(memory_space=pltpu.MemorySpace.HBM)
+    f32 = jnp.float32
+    seq_sem = pltpu.SemaphoreType.DMA((n_seq,))
+    head_sem = pltpu.SemaphoreType.DMA((n_head,))
+    near_sem = pltpu.SemaphoreType.DMA((4,))
+    return pl.pallas_call(
+        functools.partial(fused_kernel, n_seq, n_head),
+        out_shape=(block, block, block, block, jax.ShapeDtypeStruct((columns, wide), f32)),
+        in_specs=[hbm, hbm, hbm, pl.BlockSpec(memory_space=pltpu.SMEM), hbm, hbm],
+        out_specs=(vmem,) * 5,
+        scratch_shapes=[
+            pltpu.VMEM((columns, rows), f32),
+            pltpu.VMEM((columns, rows), f32),
+            pltpu.VMEM((columns, rows), f32),
+            pltpu.VMEM((columns, wide), f32),
+            pltpu.VMEM((columns, rows), f32),
+            pltpu.SemaphoreType.DMA((5,)),
+            pltpu.VMEM((1, n_seq * 8, rows), f32),
+            seq_sem, seq_sem, seq_sem, seq_sem,
+            pltpu.VMEM((n_seq // 2, chunk, wide), f32),
+            pltpu.VMEM((columns * n_head, rows), f32),
+            pltpu.VMEM((4, columns, rows), f32),
+            pltpu.VMEM((columns, rows), f32),
+            pltpu.VMEM((heads, n_seq * picked, rows), f32),
+            pltpu.VMEM((heads, n_seq * picked, rows), f32),
+            pltpu.VMEM((1, n_seq * 8, rows), f32),
+            pltpu.VMEM((columns, rows), f32),
+            pltpu.VMEM((wide, rows), f32),
+            pltpu.VMEM((n_head, columns, rows), f32),
+            pltpu.VMEM((columns, wide), f32),
+            pltpu.VMEM((n_seq // 2, chunk, wide), f32),
+            head_sem, head_sem, near_sem, near_sem, seq_sem, seq_sem, seq_sem, seq_sem,
+            seq_sem, seq_sem, seq_sem, seq_sem, seq_sem, seq_sem, head_sem, head_sem,
+        ],
+        compiler_params=pltpu.CompilerParams(
+            collective_id=0, has_side_effects=True, vmem_limit_bytes=40 * 1024 * 1024
+        ),
+    )(queries, keys, values, counts, out_weight, cotangent)
+
+
 def solution(mesh):
+    n_seq, n_head = mesh.shape["seq"], mesh.shape["head"]
+    whole_is_middle = n_seq <= 1 << LOG2_CENTRAL and n_seq % 2 == 0
+    body = functools.partial(fused, n_seq, n_head) if whole_is_middle else on_device
     in_specs = (
         P("head", "seq"),
         P("head", "seq"),
@@ -268,5 +704,5 @@
         P("head", None),
     )
     return jax.shard_map(
-        on_device, mesh=mesh, in_specs=in_specs, out_specs=out_specs, check_vma=False
-    )
+        body, mesh=mesh, in_specs=in_specs, out_specs=out_specs, check_vma=False
+    )

time: 283 us -> 57.5 us (0.20)
  blocking collectives: 125 us -> 0 us
  waiting for transfers between devices: 68.7 us -> 0 us
  Pallas kernels: 0 us -> 47.9 us
  local copies, waits for them, and re-layouts: 31.8 us -> 8 us
  between operations: 17.2 us -> 1.3 us
  starting transfers between devices: 14.3 us -> 0 us
  other arithmetic: 12.9 us -> 0 us
  matrix products: 12 us -> 0 us
    all_gather x5 -> x0, blocking collectives: 125 us -> none  [the longest x1 30.8 us: on_device(): stats_piece = lax.all_gather(far_stats, 'seq', axis=3, tiled=True)]
    pallas_call x0 -> x1, Pallas kernels: none -> 47.9 us  [fused(): pl.pallas_call(functools.partial(fused_kernel, n_seq, n_head), out_shape=...]
    psum x1 -> x0, waiting for transfers between devices: 47.7 us -> none  [on_device(): weight_grad = lax.psum(weight_local, 'seq')]
    ppermute x12 -> x0, waiting for transfers between devices: 20.9 us -> none  [from_partner(): lax.ppermute(shard, axis, [(i, i ^ 1 << apart) for i in range(lax.axis_si...]
    ppermute x12 -> x0, starting transfers between devices: 14.3 us -> none  [from_partner(): lax.ppermute(shard, axis, [(i, i ^ 1 << apart) for i in range(lax.axis_si...]
    dot_general x23 -> x0, matrix products: 12 us -> none  [the longest x2 1.93 us: on_device(): jnp.einsum('hqk,hek->heq', score_grads, key_rows, precision=PRECISE)]
    unnamed x133 -> x15, local copies, waits for them, and re-layouts: 18.3 us -> 8 us
    broadcast_in_dim x34 -> x0, local copies, waits for them, and re-layouts: 6.87 us -> none  [place_rows(): spread = jnp.where(chosen, piece[..., None], filler)]
  transfers between devices with their start and end apart: 14 -> 0, of which waited for: 8 -> 0; matrix products, arithmetic and copies ran while one was open for 10% -> 0% of each run, Pallas kernels for 0% -> 0%
where the time goes in v1:
time: 57.5 us; the launch traced here: 57.2 us
  Pallas kernels  47.9 us (83%)
  local copies, waits for them, and re-layouts  8 us (14%)
  between operations  1.3 us (2%)
    pallas_call x1, Pallas kernels, fused(): pl.pallas_call(functools.partial(fused_kernel, n_seq, n_head), out_shape=...  47.9 us
    unnamed x15, local copies, waits for them, and re-layouts  8 us

profile of v1, /device:TPU:0, one launch (start us, length us, event | category | flops | bytes accessed | tf_op | source)
XLA Modules:
  0.0 57.2 jit_solution(7260857787458232033)
XLA Ops:
  1.3 0.0 copy-start
  1.3 1.1 %copy-done = f32[192,768]{1,0:T(8,128)S(1)} copy-done((f32[192,768]{1,0:T(8,128)S(1)}, f32[192,768]{1,0:T(8,128)}, u32[]{:S(2)}) %copy-start) | copy-done | bytes 589848
  2.3 0.0 copy-start.1
  2.3 0.9 %copy-done.1 = f32[192,128]{1,0:T(8,128)S(1)} copy-done((f32[192,128]{1,0:T(8,128)S(1)}, f32[192,128]{1,0:T(8,128)}, u32[]{:S(2)}) %copy-start.1) | copy-done | bytes 98328
  3.2 0.0 copy-start.2
  3.2 0.9 %copy-done.2 = f32[192,128]{1,0:T(8,128)S(1)} copy-done((f32[192,128]{1,0:T(8,128)S(1)}, f32[192,128]{1,0:T(8,128)}, u32[]{:S(2)}) %copy-start.2) | copy-done | bytes 98328
  4.1 0.0 copy-start.3
  4.1 0.9 %copy-done.3 = f32[192,128]{1,0:T(8,128)S(1)} copy-done((f32[192,128]{1,0:T(8,128)S(1)}, f32[192,128]{1,0:T(8,128)}, u32[]{:S(2)}) %copy-start.3) | copy-done | bytes 98328
  5.0 0.0 copy-start.4
  5.0 0.9 %copy-done.4 = f32[192,128]{1,0:T(8,128)S(1)} copy-done((f32[192,128]{1,0:T(8,128)S(1)}, f32[192,128]{1,0:T(8,128)}, u32[]{:S(2)}) %copy-start.4) | copy-done | bytes 98328
  5.9 47.9 %shard_map.101 = (f32[192,128]{1,0:T(8,128)S(1)}, f32[192,128]{1,0:T(8,128)S(1)}, f32[192,128]{1,0:T(8,128)S(1)}, f32[192,128]{1,0:T(8,128)S(1)}, f32[192,768]{1,0:T(8,128)S(1)}) custom-call(f32[192,128]{1,0:T(8,128)S(1)} %copy-done.1, f32[192,128]{1,0:T(8,128)S(1)} %copy-done.2, f32[192,128]{1,0:T(8,128)S(1)} %copy-done.3, s32[1]{0:T(128)S(6)} %copy.16.count_ref, ...), custom_call_target="tpu_custom_call" | custom-call | tf_op jit(solution)/shard_map/pallas_call | solution.py:652
  53.8 0.6 %copy.17 = f32[192,128]{1,0:T(8,128)} copy(f32[192,128]{1,0:T(8,128)S(1)} %get-tuple-element.10) | data formatting | bytes 196608
  54.5 0.6 %copy.18 = f32[192,128]{1,0:T(8,128)} copy(f32[192,128]{1,0:T(8,128)S(1)} %get-tuple-element.11) | data formatting | bytes 196608
  55.1 0.6 %copy.19 = f32[192,128]{1,0:T(8,128)} copy(f32[192,128]{1,0:T(8,128)S(1)} %get-tuple-element.12) | data formatting | bytes 196608
  55.8 0.6 %copy.20 = f32[192,128]{1,0:T(8,128)} copy(f32[192,128]{1,0:T(8,128)S(1)} %get-tuple-element.13) | data formatting | bytes 196608
  56.4 0.8 %copy.21 = f32[192,768]{1,0:T(8,128)} copy(f32[192,768]{1,0:T(8,128)S(1)} %get-tuple-element.14) | data formatting | bytes 1179648
Async XLA Ops:
  1.3 1.1 %copy-start = (f32[192,768]{1,0:T(8,128)S(1)}, f32[192,768]{1,0:T(8,128)}, u32[]{:S(2)}) copy-start(f32[192,768]{1,0:T(8,128)} %w_hbm.1) | copy-start | bytes 1769476
  2.3 0.9 %copy-start.1 = (f32[192,128]{1,0:T(8,128)S(1)}, f32[192,128]{1,0:T(8,128)}, u32[]{:S(2)}) copy-start(f32[192,128]{1,0:T(8,128)} %q_hbm.1) | copy-start | bytes 294916
  3.2 0.9 %copy-start.2 = (f32[192,128]{1,0:T(8,128)S(1)}, f32[192,128]{1,0:T(8,128)}, u32[]{:S(2)}) copy-start(f32[192,128]{1,0:T(8,128)} %k_hbm.1) | copy-start | bytes 294916
  4.1 0.9 %copy-start.3 = (f32[192,128]{1,0:T(8,128)S(1)}, f32[192,128]{1,0:T(8,128)}, u32[]{:S(2)}) copy-start(f32[192,128]{1,0:T(8,128)} %v_hbm.1) | copy-start | bytes 294916
  5.0 0.9 %copy-start.4 = (f32[192,128]{1,0:T(8,128)S(1)}, f32[192,128]{1,0:T(8,128)}, u32[]{:S(2)}) copy-start(f32[192,128]{1,0:T(8,128)} %cot_hbm.1) | copy-start | bytes 294916

commit v2 on v1

--- a/solution.py
+++ b/solution.py
@@ -679,7 +679,7 @@
             seq_sem, seq_sem, seq_sem, seq_sem, seq_sem, seq_sem, head_sem, head_sem,
         ],
         compiler_params=pltpu.CompilerParams(
-            collective_id=0, has_side_effects=True, vmem_limit_bytes=40 * 1024 * 1024
+            collective_id=0, has_side_effects=True, vmem_limit_bytes=60 * 1024 * 1024
         ),
     )(queries, keys, values, counts, out_weight, cotangent)
 

time: 57.5 us -> 56.9 us (0.990)
  local copies, waits for them, and re-layouts: 8 us -> 7.03 us
    unnamed x15 -> x7, local copies, waits for them, and re-layouts: 8 us -> 7.03 us
where the time goes in v2:
time: 56.9 us; the launch traced here: 56.6 us
  Pallas kernels  48.3 us (85%)
  local copies, waits for them, and re-layouts  7.03 us (12%)
  between operations  1.3 us (2%)
    pallas_call x1, Pallas kernels, fused(): pl.pallas_call(functools.partial(fused_kernel, n_seq, n_head), out_shape=...  48.3 us
    unnamed x7, local copies, waits for them, and re-layouts  7.03 us

profile of v2, /device:TPU:0, one launch (start us, length us, event | category | flops | bytes accessed | tf_op | source)
XLA Modules:
  0.0 56.6 jit_solution(12390316693823743995)
XLA Ops:
  1.3 48.3 %shard_map.101 = (f32[192,128]{1,0:T(8,128)}, f32[192,128]{1,0:T(8,128)}, f32[192,128]{1,0:T(8,128)}, f32[192,128]{1,0:T(8,128)}, f32[192,768]{1,0:T(8,128)}) custom-call(f32[192,128]{1,0:T(8,128)} %q_hbm.1, f32[192,128]{1,0:T(8,128)} %k_hbm.1, f32[192,128]{1,0:T(8,128)} %v_hbm.1, s32[1]{0:T(128)S(6)} %copy.16.count_ref, f32[192,768]{1,0:T(8,128)} %w_hbm.1, ...), custom_call_target="tpu_custom_call" | custom-call | tf_op jit(solution)/shard_map/pallas_call | solution.py:652
  49.6 0.0 copy-start
  49.6 1.6 %copy.17 = f32[192,128]{1,0:T(8,128)} copy(f32[192,128]{1,0:T(8,128)} %get-tuple-element.10) | data formatting | bytes 196608
  51.2 1.5 %copy.18 = f32[192,128]{1,0:T(8,128)} copy(f32[192,128]{1,0:T(8,128)} %get-tuple-element.11) | data formatting | bytes 196608
  52.7 1.5 %copy.19 = f32[192,128]{1,0:T(8,128)} copy(f32[192,128]{1,0:T(8,128)} %get-tuple-element.12) | data formatting | bytes 196608
  54.3 1.5 %copy.20 = f32[192,128]{1,0:T(8,128)} copy(f32[192,128]{1,0:T(8,128)} %get-tuple-element.13) | data formatting | bytes 196608
  55.8 0.0 copy-done
  55.8 0.8 %copy.21 = f32[192,768]{1,0:T(8,128)} copy(f32[192,768]{1,0:T(8,128)S(1)} %copy-done) | data formatting | bytes 1179648
Async XLA Ops:
  49.6 6.2 %copy-start = (f32[192,768]{1,0:T(8,128)S(1)}, f32[192,768]{1,0:T(8,128)}, u32[]{:S(2)}) copy-start(f32[192,768]{1,0:T(8,128)} %get-tuple-element.14) | copy-start | bytes 1769476

commit v3 on v2

--- a/solution.py
+++ b/solution.py
@@ -636,6 +636,38 @@
         copy.wait_send()
 
 
+def settle_kernel(*refs):
+    count = (len(refs) - 2) // 3
+    load_sem, store_sem = refs[-2:]
+    held = refs[2 * count:3 * count]
+    loads = [
+        pltpu.make_async_copy(refs[i], held[i], load_sem.at[i]) for i in range(count)
+    ]
+    stores = [
+        pltpu.make_async_copy(held[i], refs[count + i], store_sem.at[i]) for i in range(count)
+    ]
+    for load in loads:
+        load.start()
+    for load, store in zip(loads, stores):
+        load.wait()
+        store.start()
+    for store in stores:
+        store.wait()
+
+
+def settle(arrays):
+    hbm = pl.BlockSpec(memory_space=pltpu.MemorySpace.HBM)
+    return pl.pallas_call(
+        settle_kernel,
+        out_shape=tuple(jax.ShapeDtypeStruct(a.shape, a.dtype) for a in arrays),
+        in_specs=[hbm] * len(arrays),
+        out_specs=(hbm,) * len(arrays),
+        scratch_shapes=[pltpu.VMEM(a.shape, a.dtype) for a in arrays]
+        + [pltpu.SemaphoreType.DMA((len(arrays),))] * 2,
+        compiler_params=pltpu.CompilerParams(vmem_limit_bytes=60 * 1024 * 1024),
+    )(*arrays)
+
+
 def fused(n_seq, n_head, queries, keys, values, counts, out_weight, cotangent):
     columns, rows = queries.shape
     wide = out_weight.shape[1]
@@ -649,7 +681,7 @@
     seq_sem = pltpu.SemaphoreType.DMA((n_seq,))
     head_sem = pltpu.SemaphoreType.DMA((n_head,))
     near_sem = pltpu.SemaphoreType.DMA((4,))
-    return pl.pallas_call(
+    results = pl.pallas_call(
         functools.partial(fused_kernel, n_seq, n_head),
         out_shape=(block, block, block, block, jax.ShapeDtypeStruct((columns, wide), f32)),
         in_specs=[hbm, hbm, hbm, pl.BlockSpec(memory_space=pltpu.SMEM), hbm, hbm],
@@ -682,6 +714,7 @@
             collective_id=0, has_side_effects=True, vmem_limit_bytes=60 * 1024 * 1024
         ),
     )(queries, keys, values, counts, out_weight, cotangent)
+    return settle(results)
 
 
 def solution(mesh):

time: 56.9 us -> 51.9 us (0.912)
  local copies, waits for them, and re-layouts: 7.03 us -> 0 us
  Pallas kernels: 48.3 us -> 50.5 us
    unnamed x7 -> x0, local copies, waits for them, and re-layouts: 7.03 us -> none
    pallas_call x0 -> x1, Pallas kernels: none -> 2.17 us  [settle(): pl.pallas_call(settle_kernel, out_shape=tuple((jax.ShapeDtypeStruct(a.sha...]
where the time goes in v3:
time: 51.9 us; the launch traced here: 51.8 us
  Pallas kernels  50.5 us (97%)
  between operations  1.29 us (2%)
    pallas_call x1, Pallas kernels, fused(): pl.pallas_call(functools.partial(fused_kernel, n_seq, n_head), out_shape=...  48.3 us
    pallas_call x1, Pallas kernels, settle(): pl.pallas_call(settle_kernel, out_shape=tuple((jax.ShapeDtypeStruct(a.sha...  2.17 us

profile of v3, /device:TPU:0, one launch (start us, length us, event | category | flops | bytes accessed | tf_op | source)
XLA Modules:
  0.0 51.8 jit_solution(11960145293658030511)
XLA Ops:
  1.3 48.3 %shard_map.101 = (f32[192,128]{1,0:T(8,128)}, f32[192,128]{1,0:T(8,128)}, f32[192,128]{1,0:T(8,128)}, f32[192,128]{1,0:T(8,128)}, f32[192,768]{1,0:T(8,128)}) custom-call(f32[192,128]{1,0:T(8,128)} %q_hbm.1, f32[192,128]{1,0:T(8,128)} %k_hbm.1, f32[192,128]{1,0:T(8,128)} %v_hbm.1, s32[1]{0:T(128)S(6)} %copy.11.count_ref, f32[192,768]{1,0:T(8,128)} %w_hbm.1, ...), custom_call_target="tpu_custom_call" | custom-call | tf_op jit(solution)/shard_map/pallas_call | solution.py:684
  49.6 2.2 %shard_map.102 = (f32[192,128]{1,0:T(8,128)}, f32[192,128]{1,0:T(8,128)}, f32[192,128]{1,0:T(8,128)}, f32[192,128]{1,0:T(8,128)}, f32[192,768]{1,0:T(8,128)}) custom-call(f32[192,128]{1,0:T(8,128)} %get-tuple-element.10.refs_0_, f32[192,128]{1,0:T(8,128)} %get-tuple-element.11.refs_1_, f32[192,128]{1,0:T(8,128)} %get-tuple-element.12.refs_2_, ...), custom_call_target="tpu_custom_call" | custom-call | tf_op jit(solution)/shard_map/pallas_call | solution.py:660

commit v4 on v3

--- a/solution.py
+++ b/solution.py
@@ -504,8 +504,6 @@
         stat_rows.append(lse)
         delta_rows.append(delta)
         kept.append((km, vm, pm, p0, p1, delta, far_slot, in_mid, in_far))
-        if h == 0:
-            sent += forward(qdm, send_qd, recv_qd)
     stat_slot = lax.broadcasted_iota(jnp.int32, (8, rows), 0)
     dense = jnp.zeros((8, rows), jnp.float32)
     for i, row in enumerate(stat_rows + delta_rows):
@@ -524,6 +522,7 @@
         copy.start()
         sent.append(copy)
     sent += spread(stats, send_st, recv_st, 8)
+    sent += forward(qdm, send_qd, recv_qd)
     terms[...] = product(w_ref[...], attended[...], TN)
     for k in range(1, n_head):
         copy = over_head(

time: 51.9 us -> 48.8 us (0.940)
  Pallas kernels: 50.5 us -> 47.3 us
    pallas_call x1, Pallas kernels: 48.3 us -> 45.2 us  [fused(): pl.pallas_call(functools.partial(fused_kernel, n_seq, n_head), out_shape=...]
where the time goes in v4:
time: 48.8 us; the launch traced here: 48.6 us
  Pallas kernels  47.3 us (97%)
  between operations  1.29 us (3%)
    pallas_call x1, Pallas kernels, fused(): pl.pallas_call(functools.partial(fused_kernel, n_seq, n_head), out_shape=...  45.2 us
    pallas_call x1, Pallas kernels, settle(): pl.pallas_call(settle_kernel, out_shape=tuple((jax.ShapeDtypeStruct(a.sha...  2.17 us

profile of v4, /device:TPU:0, one launch (start us, length us, event | category | flops | bytes accessed | tf_op | source)
XLA Modules:
  0.0 48.6 jit_solution(8010713351510421908)
XLA Ops:
  1.3 45.2 %shard_map.101 = (f32[192,128]{1,0:T(8,128)}, f32[192,128]{1,0:T(8,128)}, f32[192,128]{1,0:T(8,128)}, f32[192,128]{1,0:T(8,128)}, f32[192,768]{1,0:T(8,128)}) custom-call(f32[192,128]{1,0:T(8,128)} %q_hbm.1, f32[192,128]{1,0:T(8,128)} %k_hbm.1, f32[192,128]{1,0:T(8,128)} %v_hbm.1, s32[1]{0:T(128)S(6)} %copy.11.count_ref, f32[192,768]{1,0:T(8,128)} %w_hbm.1, ...), custom_call_target="tpu_custom_call" | custom-call | tf_op jit(solution)/shard_map/pallas_call | solution.py:683
  46.5 2.2 %shard_map.102 = (f32[192,128]{1,0:T(8,128)}, f32[192,128]{1,0:T(8,128)}, f32[192,128]{1,0:T(8,128)}, f32[192,128]{1,0:T(8,128)}, f32[192,768]{1,0:T(8,128)}) custom-call(f32[192,128]{1,0:T(8,128)} %get-tuple-element.10.refs_0_, f32[192,128]{1,0:T(8,128)} %get-tuple-element.11.refs_1_, f32[192,128]{1,0:T(8,128)} %get-tuple-element.12.refs_2_, ...), custom_call_target="tpu_custom_call" | custom-call | tf_op jit(solution)/shard_map/pallas_call | solution.py:659
